TPU v7x, 128 devices: a whole 4x4x4 slice. The times are simulated.
128 devices in a mesh: ctx: 16 (over y_lo, z, core), head: 8 (over x, y_hi).
Axes of the slice: x: 4, y: 4 (y_hi: 2, y_lo: 2; y = y_hi * 2 + y_lo), z: 4, core: 2. Of those that a mesh axis runs over, the one named last changes fastest.
Arguments:
- queries: bfloat16 [2048, 36864], P('ctx', 'head'), may hold values from -296 to 296
- latent_keys: bfloat16 [2048, 576], P('ctx'), may hold values from -9 to 9
- block_order: int32 [16], replicated, may hold values from 0 to 15, each once
- out_grad: bfloat16 [2048, 32768], P('ctx', 'head'), may hold values from -6 to 6
Outputs:
- attended: bfloat16 [2048, 32768], P('ctx', 'head')
- query_grad: bfloat16 [2048, 36864], P('ctx', 'head')
- latent_grad: bfloat16 [2048, 576], P('ctx')
Inputs may be any that keep to these rules, and one draw needn't show every extreme that they name: `block_order`: a permutation: each block index once.
All inputs are finite; a program needn't handle non-finite values.
Results may differ from a plain program's by a relative error of at most 0.034.
Values may be sent and summed in bfloat16 or wider, within the bound.
A program may use at most 64 MiB of HBM per device.

v0:
```python
import jax
import jax.numpy as jnp
from jax import lax
from jax.sharding import PartitionSpec as P

LATENT = 512
ROPE = 64
score_scale = 192.0 ** (-0.5)
masked_value = -1e30


def row_positions(block_order, first_row, count, shard_rows):
    rows = first_row + jnp.arange(count, dtype=jnp.int32)
    owner = rows // shard_rows
    blocks = block_order.shape[0]
    onehot = (owner[:, None] == jnp.arange(blocks, dtype=jnp.int32)[None, :]).astype(jnp.int32)
    base = jnp.sum(onehot * block_order[None, :], axis=1)
    return base * shard_rows + rows % shard_rows


def local(queries, latent_keys, block_order, out_grad):
    kdim = LATENT + ROPE
    shard_rows = latent_keys.shape[0]
    head_count = queries.shape[1] // kdim
    query_three = queries.reshape(shard_rows, head_count, kdim)
    grad_three = out_grad.reshape(shard_rows, head_count, LATENT)
    own_index = lax.axis_index("ctx")
    query_pos = row_positions(block_order, own_index * shard_rows, shard_rows, shard_rows)

    def piece_scores(piece, start):
        score = (
            jnp.einsum("thd,pd->htp", query_three, piece, preferred_element_type=jnp.float32)
            * score_scale
        )
        key_pos = row_positions(block_order, start, piece.shape[0], shard_rows)
        visible = key_pos[None, :] <= query_pos[:, None]
        return (jnp.where(visible[None], score, masked_value), visible)

    running_max = jnp.full((head_count, shard_rows), masked_value, jnp.float32)
    score, visible = piece_scores(
        lax.all_gather(latent_keys, "ctx", axis=0, tiled=True), jnp.int32(0)
    )
    new_max = jnp.maximum(running_max, jnp.max(score, axis=2))
    weights = jnp.where(visible[None], jnp.exp(score - new_max[:, :, None]), 0.0)
    new_sum = jnp.sum(weights, axis=2)
    lse = new_max + jnp.log(new_sum)
    piece = lax.all_gather(latent_keys, "ctx", axis=0, tiled=True)
    score, visible = piece_scores(piece, jnp.int32(0))
    prob_b = jnp.where(visible[None], jnp.exp(score - lse[:, :, None]), 0.0).astype(jnp.bfloat16)
    accum = jnp.einsum("htp,pe->the", prob_b, piece[:, :LATENT], preferred_element_type=jnp.float32)
    attended = accum.astype(jnp.bfloat16)
    delta = jnp.sum(attended.astype(jnp.float32) * grad_three.astype(jnp.float32), axis=2).T
    piece = lax.all_gather(latent_keys, "ctx", axis=0, tiled=True)
    score, visible = piece_scores(piece, jnp.int32(0))
    prob = jnp.where(visible[None], jnp.exp(score - lse[:, :, None]), 0.0)
    prob_b = prob.astype(jnp.bfloat16)
    dprob = jnp.einsum(
        "the,pe->htp", grad_three, piece[:, :LATENT], preferred_element_type=jnp.float32
    )
    dscore = (prob * (dprob - delta[:, :, None])).astype(jnp.bfloat16)
    query_accum = jnp.einsum("htp,pd->thd", dscore, piece, preferred_element_type=jnp.float32)
    key_part = score_scale * jnp.einsum(
        "htp,thd->pd", dscore, query_three, preferred_element_type=jnp.float32
    )
    value_part = jnp.einsum("htp,the->pe", prob_b, grad_three, preferred_element_type=jnp.float32)
    term = key_part + jnp.pad(value_part, ((0, 0), (0, ROPE)))
    key_accum = term
    query_accum, key_accum = (query_accum, key_accum)
    query_grad = (
        (score_scale * query_accum).astype(jnp.bfloat16).reshape(shard_rows, head_count * kdim)
    )
    partial_rows = lax.psum_scatter(key_accum, "ctx", scatter_dimension=0, tiled=True)
    latent_grad = lax.psum(partial_rows, "head").astype(jnp.bfloat16)
    return (attended.reshape(shard_rows, head_count * LATENT), query_grad, latent_grad)


def solution(mesh):
    placed = (P("ctx", "head"), P("ctx", None), P(), P("ctx", "head"))
    return jax.shard_map(
        local,
        mesh=mesh,
        in_specs=placed,
        out_specs=(P("ctx", "head"), P("ctx", "head"), P("ctx", None)),
        check_vma=False,
    )
```

profile of v0, /device:TPU:0, one launch (start us, length us, event | category | flops | bytes accessed | tf_op | source)
XLA Modules:
  0.0 196.5 jit_solution(11976603212448171671)
XLA Ops:
  7.2 0.0 copy-start
  7.2 0.0 copy-start.3
  7.2 0.0 all-gather.2.cloned.1.call-start
  7.2 0.7 all-gather.2.cloned.1.call-update
  7.9 0.0 reduce-scatter.2.cloned.1.call-start
  8.0 1.6 copy.34
  9.6 1.3 copy.37
  10.9 0.0 copy-done
  10.9 0.7 copy.30
  11.7 0.0 copy-done.3
  11.7 0.1 select_reduce_fusion.2
  11.8 0.1 select_reduce_fusion.1
  11.9 0.3 broadcast_compare_fusion
  12.2 38.2 %all-gather.2.cloned.1.call-done = bf16[2048,576]{0,1:T(8,128)(2,1)} async-done(((bf16[128,576]{0,1:T(8,128)(2,1)}), bf16[2048,576]{0,1:T(8,128)(2,1)}) %all-gather.2.cloned.1.call-update) | async-done | bytes 2359312 | tf_op jit(solution)/shard_map/all_gather | solution.py:47
  50.5 5.6 %fusion.3 = (f32[8,128]{1,0:T(8,128)S(1)}, f32[2048,128,8]{1,0,2:T(8,128)S(1)}) fusion(pred[128,2048]{0,1:T(8,128)(4,1)S(1)} %broadcast_compare_fusion, bf16[128,8,576]{0,2,1:T(8,128)(2,1)S(1)} %bitcast.65, bf16[2048,576]{0,1:T(8,128)(2,1)} %all-gather.2.cloned.1.call-done), kind=kOutput, calls=%fused_computation.7 | convolution fusion | flops 2422209536 | bytes 12193792 | tf_op jit(solution)/shard_map/thd,pd->htp/dot_general | solution.py:32
  56.1 2.0 %select_reduce_fusion = f32[8,128]{1,0:T(8,128)S(1)} fusion(f32[2048,128,8]{1,0,2:T(8,128)S(1)} %get-tuple-element.13, f32[8,128]{1,0:T(8,128)S(1)} %broadcast_maximum_fusion, pred[128,2048]{0,1:T(8,128)(4,1)S(1)} %broadcast_compare_fusion), kind=kLoop, calls=%fused_computation.5 | loop fusion | flops 10484736 | bytes 8658944 | tf_op jit(solution)/shard_map/reduce_sum | solution.py:45
  58.1 0.0 copy-start.1
  58.2 0.0 copy-start.4
  58.2 2.7 %convolution_bitcast_fusion = f32[2048,512]{0,1:T(8,128)S(1)} fusion(bf16[128,8,512]{0,2,1:T(8,128)(2,1)S(1)} %bitcast.62, f32[2048,128,8]{1,0,2:T(8,128)S(1)} %get-tuple-element.13, f32[8,128]{1,0:T(8,128)S(1)} %log_add_fusion, pred[128,2048]{0,1:T(8,128)(4,1)S(1)} %broadcast_compare_fusion), kind=kOutput, calls=%fused_computation.10 | convolution fusion | flops 2157969408 | bytes 13897728 | tf_op jit(solution)/shard_map/htp,the->pe/dot_general | solution.py:65
  60.9 0.0 copy-done.1
  60.9 3.7 %multiply_reduce_fusion = (f32[128,8]{0,1:T(8,128)S(1)}, bf16[128,8,512]{2,0,1:T(8,128)(2,1)}) fusion(bf16[128,8,512]{2,0,1:T(8,128)(2,1)S(1)} %copy-done.1, bf16[2048,576]{0,1:T(8,128)(2,1)S(1)} %copy-done.4, f32[2048,128,8]{1,0,2:T(8,128)S(1)} %get-tuple-element.13, f32[8,128]{1,0:T(8,128)S(1)} %log_add_fusion, ...), kind=kOutput, calls=%fused_computation.17 | convolution fusion | flops 2160589824 | bytes 12853248 | tf_op jit(solution)/shard_map/htp,pe->the/dot_general | solution.py:50
  64.6 4.5 %fusion.1 = bf16[8,128,2048]{1,2,0:T(8,128)(2,1)S(1)} fusion(f32[2048,128,8]{1,0,2:T(8,128)S(1)} %get-tuple-element.13, bf16[128,8,512]{0,2,1:T(8,128)(2,1)S(1)} %bitcast.63, f32[8,128]{1,0:T(8,128)S(1)} %bitcast.68, f32[8,128]{1,0:T(8,128)S(1)} %log_add_fusion, pred[128,2048]{0,1:T(8,128)(4,1)S(1)} %broadcast_compare_fusion, bf16[2048,576]{0,1:T(8,128)(2,1)S(1)} %copy-done.4), kind=kOutput, calls=%fused_computation.2 | convolution fusion | flops 2162163712 | bytes 15998976 | tf_op jit(solution)/shard_map/the,pe->htp/dot_general | solution.py:57
  69.0 2.0 %copy-done.5 = bf16[8,128,2048]{1,2,0:T(8,128)(2,1)} copy-done((bf16[8,128,2048]{1,2,0:T(8,128)(2,1)}, bf16[8,128,2048]{1,2,0:T(8,128)(2,1)S(1)}, u32[]{:S(2)}) %copy-start.5) | copy-done | bytes 4194328
  71.0 4.3 %fusion.4 = f32[2048,576]{0,1:T(8,128)} fusion(f32[2048,512]{0,1:T(8,128)S(1)} %convolution_bitcast_fusion, bf16[8,128,2048]{1,2,0:T(8,128)(2,1)S(1)} %fusion.1, bf16[128,8,576]{0,2,1:T(8,128)(2,1)S(1)} %bitcast.66), kind=kOutput, calls=%fused_computation.9 | convolution fusion | flops 2418278400 | bytes 14286848 | tf_op jit(solution)/shard_map/htp,thd->pd/dot_general | solution.py:62
  75.4 0.0 reduce-scatter.2.cloned.1.call-update
  75.4 1.2 copy-done.2
  76.6 0.7 copy.33
  77.2 1.3 copy.41
  78.6 5.5 %multiply_convert_fusion = bf16[8,128,576]{1,2,0:T(8,128)(2,1)S(1)} fusion(bf16[8,128,2048]{1,2,0:T(8,128)(2,1)} %copy-done.5, bf16[2048,576]{0,1:T(8,128)(2,1)} %all-gather.2.cloned.1.call-done), kind=kOutput, calls=%fused_computation.15 | convolution fusion | flops 2417098752 | bytes 7733248 | tf_op jit(solution)/shard_map/htp,pd->thd/dot_general | solution.py:61
  84.1 1.4 copy.42
  85.5 58.2 %reduce-scatter.2.cloned.1.call-done = f32[128,576]{0,1:T(8,128)} async-done(((f32[2048,576]{0,1:T(8,128)}), f32[128,576]{0,1:T(8,128)}) %reduce-scatter.2.cloned.1.call-update) | async-done | bytes 294928 | tf_op jit(solution)/shard_map/reduce_scatter | solution.py:72
  143.7 45.9 %all-reduce.2 = bf16[128,576]{0,1:T(8,128)(2,1)} all-reduce(f32[128,576]{0,1:T(8,128)} %reduce-scatter.2.cloned.1.call-done), channel_id=1, replica_groups=mesh['ctx'=16,'head'=8] {'head'}, use_global_device_ids=true, to_apply=%region_6.7 | all-reduce | flops 73728 | bytes 442368 | tf_op jit(solution)/shard_map/psum | solution.py:73
  (9 shorter events, 0.1 us)
Async XLA Ops:
  7.2 3.7 %copy-start = (bf16[128,4608]{1,0:T(8,128)(2,1)S(1)}, bf16[128,4608]{1,0:T(8,128)(2,1)}, u32[]{:S(2)}) copy-start(bf16[128,4608]{1,0:T(8,128)(2,1)} %param.4) | copy-start | bytes 3538948
  7.2 4.5 %copy-start.3 = (s32[16]{0:T(128)S(1)}, s32[16]{0:T(128)}, u32[]{:S(2)}) copy-start(s32[16]{0:T(128)} %param.6) | copy-start | bytes 196
  7.2 43.3 %all-gather.2.cloned.1.call-start = ((), (), s32[]{:S(2)}) async-start(), calls=%async_computation.1 | async-start | bytes 2506752 | tf_op jit(solution)/shard_map/all_gather | solution.py:47
  7.9 135.8 %reduce-scatter.2.cloned.1.call-start = ((), (), s32[]{:S(2)}) async-start(), calls=%async_computation.2 | async-start | bytes 5013504 | tf_op jit(solution)/shard_map/reduce_scatter | solution.py:72
  58.1 2.7 %copy-start.1 = (bf16[128,8,512]{2,0,1:T(8,128)(2,1)S(1)}, bf16[128,8,512]{2,0,1:T(8,128)(2,1)}, u32[]{:S(2)}) copy-start(bf16[128,8,512]{2,0,1:T(8,128)(2,1)} %copy.37) | copy-start | bytes 3145732
  58.2 2.7 %copy-start.4 = (bf16[2048,576]{0,1:T(8,128)(2,1)S(1)}, bf16[2048,576]{0,1:T(8,128)(2,1)}, u32[]{:S(2)}) copy-start(bf16[2048,576]{0,1:T(8,128)(2,1)} %all-gather.2.cloned.1.call-done) | copy-start | bytes 7077892
  69.0 2.0 %copy-start.5 = (bf16[8,128,2048]{1,2,0:T(8,128)(2,1)}, bf16[8,128,2048]{1,2,0:T(8,128)(2,1)S(1)}, u32[]{:S(2)}) copy-start(bf16[8,128,2048]{1,2,0:T(8,128)(2,1)S(1)} %fusion.1) | copy-start | bytes 12582916
  75.4 1.2 copy-start.2
Sparse Core Ops, SparseCore 0:
  9.6 40.7 all-gather.1
  75.5 68.1 reduce-scatter.1
where the time goes:
time: 197 us; the launch traced here: 196 us
  waiting for transfers between devices  97.2 us (49%)
  blocking collectives  45.9 us (23%)
  matrix products  26.2 us (13%)
  between operations  14.2 us (7%)
  local copies, waits for them, and re-layouts  10.3 us (5%)
  other arithmetic  2.6 us (1%)
    reduce_scatter x1, waiting for transfers between devices, local(): lax.psum_scatter(key_accum, 'ctx', scatter_dimension=0, tiled=True)  58.2 us
    psum x1, blocking collectives, local(): latent_grad = lax.psum(partial_rows, 'head').astype(jnp.bfloat16)  45.9 us
    all_gather x1, waiting for transfers between devices, local(): piece = lax.all_gather(latent_keys, 'ctx', axis=0, tiled=True)  38.2 us
    unnamed x16, local copies, waits for them, and re-layouts  8.29 us
    dot_general x1, matrix products, piece_scores(): jnp.einsum('thd,pd->htp', query_three, piece, preferred_element_type=jnp....  5.59 us
    dot_general x1, matrix products, local(): jnp.einsum('htp,pd->thd', dscore, piece, preferred_element_type=jnp.float32)  5.5 us
    dot_general x1, matrix products, local(): jnp.einsum('the,pe->htp', grad_three, piece[:, :LATENT], preferred_elemen...  4.47 us
    dot_general x1, matrix products, local(): jnp.einsum('htp,thd->pd', dscore, query_three, preferred_element_type=jnp...  4.31 us
  transfers between devices with their start and end apart: 2, of which 2 were waited for; matrix products, arithmetic and copies ran while one was open for 7% of the time, Pallas kernels for 0%

commit v1 on v0

--- a/solution.py
+++ b/solution.py
@@ -70,7 +70,7 @@
         (score_scale * query_accum).astype(jnp.bfloat16).reshape(shard_rows, head_count * kdim)
     )
     partial_rows = lax.psum_scatter(key_accum, "ctx", scatter_dimension=0, tiled=True)
-    latent_grad = lax.psum(partial_rows, "head").astype(jnp.bfloat16)
+    latent_grad = jnp.sum(lax.all_gather(partial_rows, "head"), axis=0).astype(jnp.bfloat16)
     return (attended.reshape(shard_rows, head_count * LATENT), query_grad, latent_grad)
 
 

time: 197 us -> 215 us (1.091)
  waiting for transfers between devices: 97.2 us -> 159 us
  blocking collectives: 45.9 us -> 0 us
    all_gather x0 -> x1, waiting for transfers between devices: none -> 51.7 us  [local(): lax.all_gather(partial_rows, 'head')]
    psum x1 -> x0, blocking collectives: 45.9 us -> none  [local(): latent_grad = lax.psum(partial_rows, 'head').astype(jnp.bfloat16)]
    reduce_scatter x1, waiting for transfers between devices: 58.2 us -> 68.3 us  [local(): lax.psum_scatter(key_accum, 'ctx', scatter_dimension=0, tiled=True)]
    unnamed x16 -> x17, local copies, waits for them, and re-layouts: 8.29 us -> 9.29 us
  transfers between devices with their start and end apart: 2 -> 3, of which waited for: 2 -> 3; matrix products, arithmetic and copies ran while one was open for 7% -> 6% of each run, Pallas kernels for 0% -> 0%
where the time goes in v1:
time: 215 us; the launch traced here: 214 us
  waiting for transfers between devices  159 us (74%)
  matrix products  26.2 us (12%)
  between operations  13.9 us (6%)
  local copies, waits for them, and re-layouts  11.3 us (5%)
  other arithmetic  3.9 us (2%)
    reduce_scatter x1, waiting for transfers between devices, local(): lax.psum_scatter(key_accum, 'ctx', scatter_dimension=0, tiled=True)  68.3 us
    all_gather x1, waiting for transfers between devices, local(): lax.all_gather(partial_rows, 'head')  51.7 us
    all_gather x1, waiting for transfers between devices, local(): piece = lax.all_gather(latent_keys, 'ctx', axis=0, tiled=True)  38.2 us
    unnamed x17, local copies, waits for them, and re-layouts  9.29 us
    dot_general x1, matrix products, piece_scores(): jnp.einsum('thd,pd->htp', query_three, piece, preferred_element_type=jnp....  5.59 us
    dot_general x1, matrix products, local(): jnp.einsum('htp,pd->thd', dscore, piece, preferred_element_type=jnp.float32)  5.5 us
    dot_general x1, matrix products, local(): jnp.einsum('the,pe->htp', grad_three, piece[:, :LATENT], preferred_elemen...  4.47 us
    dot_general x1, matrix products, local(): jnp.einsum('htp,thd->pd', dscore, query_three, preferred_element_type=jnp...  4.31 us
  transfers between devices with their start and end apart: 3, of which 3 were waited for; matrix products, arithmetic and copies ran while one was open for 6% of the time, Pallas kernels for 0%

profile of v1, /device:TPU:0, one launch (start us, length us, event | category | flops | bytes accessed | tf_op | source)
XLA Modules:
  0.0 214.4 jit_solution(8906080239367731311)
XLA Ops:
  7.2 0.0 copy-start
  7.2 0.0 all-gather.4.cloned.1.call-start
  7.2 0.7 all-gather.4.cloned.1.call-update
  7.9 0.0 reduce-scatter.2.cloned.1.call-start
  8.0 1.6 copy.34
  9.6 1.3 copy.37
  10.9 0.0 copy-done
  10.9 0.7 copy.30
  11.7 0.1 select_reduce_fusion.2
  11.8 0.1 select_reduce_fusion.1
  11.9 0.3 broadcast_compare_fusion
  12.2 38.2 %all-gather.4.cloned.1.call-done = bf16[2048,576]{0,1:T(8,128)(2,1)} async-done(((bf16[128,576]{0,1:T(8,128)(2,1)}), bf16[2048,576]{0,1:T(8,128)(2,1)}) %all-gather.4.cloned.1.call-update) | async-done | bytes 2359312 | tf_op jit(solution)/shard_map/all_gather | solution.py:47
  50.5 5.6 %fusion.3 = (f32[8,128]{1,0:T(8,128)S(1)}, f32[2048,128,8]{1,0,2:T(8,128)S(1)}) fusion(pred[128,2048]{0,1:T(8,128)(4,1)S(1)} %broadcast_compare_fusion, bf16[128,8,576]{0,2,1:T(8,128)(2,1)S(1)} %bitcast.71, bf16[2048,576]{0,1:T(8,128)(2,1)} %all-gather.4.cloned.1.call-done), kind=kOutput, calls=%fused_computation.7 | convolution fusion | flops 2422209536 | bytes 12193792 | tf_op jit(solution)/shard_map/thd,pd->htp/dot_general | solution.py:32
  56.1 2.0 select_reduce_fusion
  58.1 0.0 copy-start.1
  58.2 0.0 copy-start.4
  58.2 2.7 %convolution_bitcast_fusion = f32[2048,512]{0,1:T(8,128)S(1)} fusion(bf16[128,8,512]{0,2,1:T(8,128)(2,1)S(1)} %bitcast.67, f32[2048,128,8]{1,0,2:T(8,128)S(1)} %get-tuple-element.13, f32[8,128]{1,0:T(8,128)S(1)} %log_add_fusion, pred[128,2048]{0,1:T(8,128)(4,1)S(1)} %broadcast_compare_fusion), kind=kOutput, calls=%fused_computation.10 | convolution fusion | flops 2157969408 | bytes 13897728 | tf_op jit(solution)/shard_map/htp,the->pe/dot_general | solution.py:65
  60.9 3.7 %multiply_reduce_fusion = (f32[128,8]{0,1:T(8,128)S(1)}, bf16[128,8,512]{2,0,1:T(8,128)(2,1)}) fusion(bf16[128,8,512]{2,0,1:T(8,128)(2,1)S(1)} %copy-done.1, bf16[2048,576]{0,1:T(8,128)(2,1)S(1)} %copy-done.4, f32[2048,128,8]{1,0,2:T(8,128)S(1)} %get-tuple-element.13, f32[8,128]{1,0:T(8,128)S(1)} %log_add_fusion, ...), kind=kOutput, calls=%fused_computation.18 | convolution fusion | flops 2160589824 | bytes 12853248 | tf_op jit(solution)/shard_map/htp,pe->the/dot_general | solution.py:50
  64.6 4.5 %fusion.1 = bf16[8,128,2048]{1,2,0:T(8,128)(2,1)S(1)} fusion(f32[2048,128,8]{1,0,2:T(8,128)S(1)} %get-tuple-element.13, bf16[128,8,512]{0,2,1:T(8,128)(2,1)S(1)} %bitcast.68, f32[8,128]{1,0:T(8,128)S(1)} %bitcast.74, f32[8,128]{1,0:T(8,128)S(1)} %log_add_fusion, pred[128,2048]{0,1:T(8,128)(4,1)S(1)} %broadcast_compare_fusion, bf16[2048,576]{0,1:T(8,128)(2,1)S(1)} %copy-done.4), kind=kOutput, calls=%fused_computation.2 | convolution fusion | flops 2162163712 | bytes 15998976 | tf_op jit(solution)/shard_map/the,pe->htp/dot_general | solution.py:57
  69.0 2.0 copy-done.5
  71.0 4.3 %fusion.4 = f32[2048,576]{0,1:T(8,128)} fusion(f32[2048,512]{0,1:T(8,128)S(1)} %convolution_bitcast_fusion, bf16[8,128,2048]{1,2,0:T(8,128)(2,1)S(1)} %fusion.1, bf16[128,8,576]{0,2,1:T(8,128)(2,1)S(1)} %bitcast.72), kind=kOutput, calls=%fused_computation.9 | convolution fusion | flops 2418278400 | bytes 14286848 | tf_op jit(solution)/shard_map/htp,thd->pd/dot_general | solution.py:62
  75.4 0.0 reduce-scatter.2.cloned.1.call-update
  75.4 0.0 all-gather.6.cloned.1.call-start
  75.4 68.3 %reduce-scatter.2.cloned.1.call-done = f32[128,576]{0,1:T(8,128)} async-done(((f32[2048,576]{0,1:T(8,128)}), f32[128,576]{0,1:T(8,128)}) %reduce-scatter.2.cloned.1.call-update) | async-done | bytes 294928 | tf_op jit(solution)/shard_map/reduce_scatter | solution.py:72
  143.7 0.0 all-gather.6.cloned.1.call-update
  143.8 0.7 copy.33
  144.4 1.3 copy.41
  145.7 5.5 %multiply_convert_fusion = bf16[8,128,576]{1,2,0:T(8,128)(2,1)S(1)} fusion(bf16[8,128,2048]{1,2,0:T(8,128)(2,1)} %copy-done.5, bf16[2048,576]{0,1:T(8,128)(2,1)} %all-gather.4.cloned.1.call-done), kind=kOutput, calls=%fused_computation.16 | convolution fusion | flops 2417098752 | bytes 7733248 | tf_op jit(solution)/shard_map/htp,pd->thd/dot_general | solution.py:61
  151.2 1.4 copy.42
  152.7 51.7 %all-gather.6.cloned.1.call-done = f32[1024,576]{0,1:T(8,128)} async-done(((f32[128,576]{0,1:T(8,128)}), f32[1024,576]{0,1:T(8,128)}) %all-gather.6.cloned.1.call-update) | async-done | bytes 2359312 | tf_op jit(solution)/shard_map/all_gather | solution.py:73
  204.4 2.2 %copy.52 = f32[72,8,8,128]{3,2,1,0:T(8,128)S(1)} copy(f32[72,8,8,128]{3,1,2,0:T(8,128)} %bitcast.70) | data formatting | bytes 4718592
  206.6 1.3 bitcast_reduce_fusion
  (13 shorter events, 0.1 us)
Async XLA Ops:
  7.2 3.7 %copy-start = (bf16[128,4608]{1,0:T(8,128)(2,1)S(1)}, bf16[128,4608]{1,0:T(8,128)(2,1)}, u32[]{:S(2)}) copy-start(bf16[128,4608]{1,0:T(8,128)(2,1)} %param.4) | copy-start | bytes 3538948
  7.2 4.5 %copy-start.3 = (s32[16]{0:T(128)S(1)}, s32[16]{0:T(128)}, u32[]{:S(2)}) copy-start(s32[16]{0:T(128)} %param.6) | copy-start | bytes 196
  7.2 43.3 %all-gather.4.cloned.1.call-start = ((), (), s32[]{:S(2)}) async-start(), calls=%async_computation.1 | async-start | bytes 2506752 | tf_op jit(solution)/shard_map/all_gather | solution.py:47
  7.9 135.8 %reduce-scatter.2.cloned.1.call-start = ((), (), s32[]{:S(2)}) async-start(), calls=%async_computation.2 | async-start | bytes 5013504 | tf_op jit(solution)/shard_map/reduce_scatter | solution.py:72
  58.1 2.7 %copy-start.1 = (bf16[128,8,512]{2,0,1:T(8,128)(2,1)S(1)}, bf16[128,8,512]{2,0,1:T(8,128)(2,1)}, u32[]{:S(2)}) copy-start(bf16[128,8,512]{2,0,1:T(8,128)(2,1)} %copy.37) | copy-start | bytes 3145732
  58.2 2.7 %copy-start.4 = (bf16[2048,576]{0,1:T(8,128)(2,1)S(1)}, bf16[2048,576]{0,1:T(8,128)(2,1)}, u32[]{:S(2)}) copy-start(bf16[2048,576]{0,1:T(8,128)(2,1)} %all-gather.4.cloned.1.call-done) | copy-start | bytes 7077892
  69.0 2.0 copy-start.5
  75.4 68.4 %copy-start.2 = (bf16[128,8,512]{2,0,1:T(8,128)(2,1)S(1)}, bf16[128,8,512]{2,0,1:T(8,128)(2,1)}, u32[]{:S(2)}) copy-start(bf16[128,8,512]{2,0,1:T(8,128)(2,1)} %get-tuple-element.15) | copy-start | bytes 3145732
  75.4 129.0 %all-gather.6.cloned.1.call-start = ((), (), s32[]{:S(2)}) async-start(), calls=%async_computation.3 | async-start | bytes 2654208 | tf_op jit(solution)/shard_map/all_gather | solution.py:73
Sparse Core Ops, SparseCore 0:
  9.6 40.7 all-gather.3
  75.5 68.1 reduce-scatter.1
  145.9 58.4 all-gather.5
